TPU v7x, 32 devices: a whole 2x2x4 slice. The times are simulated.
32 devices in a mesh: parts: 2 (over x), dp: 4 (over y, core), tensor: 4 (over z).
Axes of the slice: x: 2, y: 2, z: 4, core: 2. Of those that a mesh axis runs over, the one named last changes fastest.
Arguments:
- hidden_input_rows: bfloat16 [10240, 28672], P(('parts', 'dp'), 'tensor'), parts along dimension 0, may hold values from -6 to 6
- output_gradient_rows: bfloat16 [10240, 8192], P(('parts', 'dp'), 'tensor'), parts along dimension 0, may hold values from -6 to 6
- adapter_down_matrix: bfloat16 [16, 28672], P(None, 'tensor'), may hold values from -0.03125 to 0.03125
- input_side_projection: bfloat16 [64, 28672], P(None, 'tensor'), may hold values from -0.03125 to 0.03125
- adapter_up_matrix: bfloat16 [8192, 16], P('tensor'), may hold values from -0.0625 to 0.0625
- output_side_projection: bfloat16 [64, 8192], P(None, 'tensor'), may hold values from -0.0625 to 0.0625
- projected_test_gradients: bfloat16 [4096, 2048], P('dp', 'tensor'), may hold values from -0.0078125 to 0.0078125
Outputs:
- scores: float32 [40, 4096], P(('parts', 'dp'), 'tensor'), parts along dimension 0
There are 2 independent parts, one for each index of `parts`. A program takes and returns all parts, laid end to end along the dimension named above; an argument that names none is the same for every part. Nothing has to cross between parts.
All inputs are finite; a program needn't handle non-finite values.
Results may differ from a plain program's by a relative error of at most 0.0029.
Values may be sent and summed in bfloat16 or wider, within the bound.
A program may use at most 128 MiB of HBM per device.

v0:
```python
import jax
import jax.numpy as jnp
from jax import lax
from jax.sharding import PartitionSpec as P

LEN = 256


def owned_columns(input_side, grad_side, adapter_rank_value, seqs, col_start, width):
    rows = input_side.shape[0]
    kdim = input_side.shape[1] - adapter_rank_value
    half = adapter_rank_value * kdim
    owner = jnp.arange(rows, dtype=jnp.int32) // LEN
    member = (owner[None, :] == jnp.arange(seqs, dtype=jnp.int32)[:, None]).astype(jnp.float32)
    stacked = jnp.concatenate([input_side, grad_side], 1)
    column = jnp.arange(width, dtype=jnp.int32) + col_start
    second_half = column - half
    in_first = column < half
    first_pick = jnp.where(
        in_first,
        2 * adapter_rank_value + kdim + column // adapter_rank_value,
        adapter_rank_value + kdim + second_half // kdim,
    )
    second_pick = jnp.where(
        in_first, column % adapter_rank_value, adapter_rank_value + second_half % kdim
    )
    source = jnp.arange(stacked.shape[1], dtype=jnp.int32)[:, None]
    pick_first = (source == first_pick[None, :]).astype(jnp.float32)
    pick_second = (source == second_pick[None, :]).astype(jnp.float32)
    factor_one = jnp.dot(stacked, pick_first, precision=lax.Precision.HIGHEST)
    factor_two = jnp.dot(stacked, pick_second, precision=lax.Precision.HIGHEST)
    return jnp.dot(member, factor_one * factor_two, precision=lax.Precision.HIGHEST)


def body(
    hidden_input_rows,
    output_gradient_rows,
    adapter_down_matrix,
    input_side_projection,
    adapter_up_matrix,
    output_side_projection,
    projected_test_gradients,
):
    contract = (((1,), (1,)), ((), ()))
    adapter_rank_value = adapter_down_matrix.shape[0]
    tokens_here = hidden_input_rows.shape[0]
    seqs = tokens_here // LEN
    width = projected_test_gradients.shape[1]
    left_factor = jnp.concatenate([adapter_down_matrix, input_side_projection], 0)
    right_factor = jnp.concatenate([adapter_up_matrix.T, output_side_projection], 0)
    from_input = lax.dot_general(
        hidden_input_rows, left_factor, contract, preferred_element_type=jnp.float32
    )
    from_grad = lax.dot_general(
        output_gradient_rows, right_factor, contract, preferred_element_type=jnp.float32
    )
    summed_in, summed_grad = lax.psum((from_input, from_grad), "tensor")
    columns = owned_columns(
        summed_in, summed_grad, adapter_rank_value, seqs, lax.axis_index("tensor") * width, width
    )
    example = columns.astype(jnp.bfloat16)
    partial_scores = lax.dot_general(
        example,
        lax.all_gather(projected_test_gradients, "dp", axis=0, tiled=True),
        contract,
        preferred_element_type=jnp.float32,
    )
    return lax.psum_scatter(partial_scores, "tensor", scatter_dimension=1, tiled=True)


def solution(mesh):
    return jax.shard_map(
        body,
        mesh=mesh,
        in_specs=(
            P(("parts", "dp"), "tensor"),
            P(("parts", "dp"), "tensor"),
            P(None, "tensor"),
            P(None, "tensor"),
            P("tensor", None),
            P(None, "tensor"),
            P("dp", "tensor"),
        ),
        out_specs=P(("parts", "dp"), "tensor"),
        check_vma=False,
    )
```

profile of v0, /device:TPU:0, one launch (start us, length us, event | category | flops | bytes accessed | tf_op | source)
XLA Modules:
  0.0 108.8 jit_solution(10766204382110805368)
XLA Ops:
  7.4 0.0 all-reduce.3.cloned.1.call-start
  7.4 0.0 copy-start
  7.4 0.0 copy-start.1
  7.4 5.2 %convolution_bitcast_fusion = f32[1280,80]{0,1:T(8,128)} fusion(bf16[1280,2048]{1,0:T(8,128)(2,1)} %param.8, bf16[64,2048]{1,0:T(8,128)(2,1)} %param.12, bf16[16,2048]{1,0:T(8,128)(2,1)} %bitcast.12), kind=kOutput, calls=%fused_computation.1 | convolution fusion | flops 420085760 | bytes 5980160 | tf_op jit(solution)/shard_map/dot_general | solution.py:54
  12.6 0.0 copy-done
  12.6 0.0 copy-done.1
  12.6 12.6 %convolution_bitcast_fusion.1 = f32[1280,80]{0,1:T(8,128)} fusion(bf16[1280,7168]{1,0:T(8,128)(2,1)} %param.7, bf16[64,7168]{1,0:T(8,128)(2,1)S(1)} %copy-done, bf16[16,7168]{1,0:T(8,128)(2,1)S(1)} %copy-done.1), kind=kOutput, calls=%fused_computation.2 | convolution fusion | flops 1470300160 | bytes 19906560 | tf_op jit(solution)/shard_map/dot_general | solution.py:51
  25.2 0.0 all-reduce.3.cloned.1.call-update
  25.2 0.0 all-gather.2.cloned.1.call-start
  25.3 0.5 all-gather.2.cloned.1.call-update
  25.8 0.0 reduce-scatter.2.cloned.1.call-start
  25.9 47.2 %all-reduce.3.cloned.1.call-done = (f32[1280,80]{0,1:T(8,128)}, f32[1280,80]{0,1:T(8,128)}) async-done(((f32[1280,80]{0,1:T(8,128)}, f32[1280,80]{0,1:T(8,128)}), (f32[1280,80]{0,1:T(8,128)}, f32[1280,80]{0,1:T(8,128)})) %all-reduce.3.cloned.1.call-update) | async-done | bytes 819216 | tf_op jit(solution)/shard_map/psum | solution.py:57
  73.1 1.0 constant_dynamic-update-slice_fusion.1
  74.2 1.0 constant_dynamic-update-slice_fusion
  75.2 1.3 %fusion.6 = f32[1280,512]{1,0:T(8,128)S(1)} fusion(f32[1280,160]{0,1:T(8,128)S(1)} %constant_dynamic-update-slice_fusion, s32[512]{0:T(512)S(1)} %get-tuple-element.7), kind=kOutput, calls=%fused_computation.12 | convolution fusion | flops 1258373120 | bytes 3442688 | tf_op jit(solution)/shard_map/dot_general | solution.py:30
  76.5 1.4 %convolution_multiply_fusion = f32[1280,512]{1,0:T(8,128)S(1)} fusion(f32[1280,512]{1,0:T(8,128)S(1)} %fusion.6, f32[1280,160]{0,1:T(8,128)S(1)} %constant_dynamic-update-slice_fusion, s32[512]{0:T(512)S(1)} %get-tuple-element.8), kind=kOutput, calls=%fused_computation | convolution fusion | flops 1259028480 | bytes 6064128 | tf_op jit(solution)/shard_map/dot_general | solution.py:31
  77.9 1.0 convolution_convert_fusion
  78.9 0.0 all-gather.2.cloned.1.call-done
  78.9 4.0 %fusion.28 = f32[5,4096]{1,0:T(8,128)} fusion(bf16[5,512]{1,0:T(8,128)(2,1)S(1)} %convolution_convert_fusion, bf16[4096,512]{1,0:T(8,128)(2,1)} %all-gather.2.cloned.1.call-done), kind=kOutput, calls=%fused_computation.54 | convolution fusion | flops 20971520 | bytes 4281344 | tf_op jit(solution)/shard_map/dot_general | solution.py:62
  82.9 0.0 reduce-scatter.2.cloned.1.call-update
  82.9 18.5 %reduce-scatter.2.cloned.1.call-done = f32[5,1024]{1,0:T(8,128)} async-done(((f32[5,4096]{1,0:T(8,128)}), f32[5,1024]{1,0:T(8,128)}) %reduce-scatter.2.cloned.1.call-update) | async-done | bytes 20496 | tf_op jit(solution)/shard_map/reduce_scatter | solution.py:68
  (2 shorter events, 0.0 us)
Async XLA Ops:
  7.4 65.8 %all-reduce.3.cloned.1.call-start = ((), (), s32[]{:S(2)}) async-start(), calls=%async_computation.3 | async-start | bytes 1638400 | tf_op jit(solution)/shard_map/psum | solution.py:57
  7.4 5.2 %copy-start = (bf16[64,7168]{1,0:T(8,128)(2,1)S(1)}, bf16[64,7168]{1,0:T(8,128)(2,1)}, u32[]{:S(2)}) copy-start(bf16[64,7168]{1,0:T(8,128)(2,1)} %param.10) | copy-start | bytes 2752516
  7.4 5.2 %copy-start.1 = (bf16[16,7168]{1,0:T(8,128)(2,1)S(1)}, bf16[16,7168]{1,0:T(8,128)(2,1)}, u32[]{:S(2)}) copy-start(bf16[16,7168]{1,0:T(8,128)(2,1)} %param.9) | copy-start | bytes 688132
  25.2 53.6 %all-gather.2.cloned.1.call-start = ((), (), s32[]{:S(2)}) async-start(), calls=%async_computation.1 | async-start | bytes 5242880 | tf_op jit(solution)/shard_map/all_gather | solution.py:64
  25.8 75.6 %reduce-scatter.2.cloned.1.call-start = ((), (), s32[]{:S(2)}) async-start(), calls=%async_computation.2 | async-start | bytes 163840 | tf_op jit(solution)/shard_map/reduce_scatter | solution.py:68
Sparse Core Ops, SparseCore 0:
  25.4 47.7 all-reduce.2
  83.0 18.2 reduce-scatter.1
Sparse Core Ops, SparseCore 1:
  27.3 37.0 all-gather.1
where the time goes:
time: 109 us
  waiting for transfers between devices  66.2 us (61%)
  matrix products  25.5 us (23%)
  between operations  14.9 us (14%)
  local copies, waits for them, and re-layouts  2.07 us (2%)
    psum x1, waiting for transfers between devices, body(): summed_in, summed_grad = lax.psum((from_input, from_grad), 'tensor')  47.2 us
    reduce_scatter x1, waiting for transfers between devices, body(): lax.psum_scatter(partial_scores, 'tensor', scatter_dimension=1, tiled=True)  18.5 us
    dot_general x1, matrix products, body(): lax.dot_general(hidden_input_rows, left_factor, contract, preferred_eleme...  12.6 us
    dot_general x1, matrix products, body(): lax.dot_general(output_gradient_rows, right_factor, contract, preferred_e...  5.19 us
    dot_general x1, matrix products, body(): lax.dot_general(example, lax.all_gather(projected_test_gradients, 'dp', a...  4.03 us
  transfers between devices with their start and end apart: 3, of which 2 were waited for; matrix products, arithmetic and copies ran while one was open for 5% of the time, Pallas kernels for 0%

commit v1 on v0

v1 whole, which is shorter than its diff:
```python
import functools

import jax
import jax.numpy as jnp
from jax import lax
from jax.experimental import pallas as pl
from jax.experimental.pallas import tpu as pltpu
from jax.sharding import PartitionSpec as P

LEN = 256
MESH = pl.DeviceIdType.MESH
WIRE = jnp.bfloat16
CONTRACT_LAST = (((1,), (1,)), ((), ()))
CONTRACT_FIRST = (((0,), (0,)), ((), ()))


def split(x):
    high = x.astype(jnp.bfloat16)
    return jnp.concatenate([high, (x - high.astype(jnp.float32)).astype(jnp.bfloat16)], 0)


def kernel(
    sizes,
    hidden, outgrad, down, inproj, up_t, outproj, tests,
    out,
    hid_v, grad_v, left_v, right_v, tests_v,
    own_a, own_b, send_p, recv_p, own_e, recv_e, own_s, all_s, part_s, recv_s,
    hid_sem, grad_sem, w_sem, t_sem,
    p_send, p_recv, e_send, e_recv, s_send, s_recv, o_send, o_recv,
):
    nd, nt = sizes
    rank, kdim = down.shape[0], inproj.shape[0]
    seqs = hidden.shape[0] // LEN
    block = LEN // nt
    pack = min(4, block // 16)
    width = tests.shape[1]
    rep = kdim // rank
    f32, bf16 = jnp.float32, jnp.bfloat16

    part = lax.axis_index("parts")
    d = lax.axis_index("dp")
    t = lax.axis_index("tensor")

    loads = []

    def load(src, dst, sem):
        copy = pltpu.make_async_copy(src, dst, sem)
        copy.start()
        return copy

    w_loads = [load(inproj, left_v.at[pl.ds(0, kdim)], w_sem.at[0])]
    for i in range(rep):
        w_loads.append(load(down, left_v.at[pl.ds(kdim + rank * i, rank)], w_sem.at[1 + i]))
    hid_loads, grad_loads = [], []
    for s in range(seqs):
        rows = pl.ds(s * LEN, LEN)
        hid_loads.append(load(hidden.at[rows], hid_v.at[rows], hid_sem.at[s]))
        if s == 0:
            for i in range(rep):
                w_loads.append(load(up_t, right_v.at[pl.ds(rank * i, rank)], w_sem.at[1 + rep + i]))
            w_loads.append(load(outproj, right_v.at[pl.ds(kdim, kdim)], w_sem.at[1 + 2 * rep]))
        grad_loads.append(load(outgrad.at[rows], grad_v.at[rows], grad_sem.at[s]))
    t_load = load(tests, tests_v, t_sem)

    barrier = pltpu.get_barrier_semaphore()
    for kd in range(nd):
        for kt in range(nt):
            if kd or kt:
                pl.semaphore_signal(
                    barrier, inc=1,
                    device_id=(part, lax.rem(d + kd, nd), lax.rem(t + kt, nt)),
                    device_id_type=MESH,
                )

    lane = lax.broadcasted_iota(jnp.int32, (LEN, 2 * kdim), 1)
    low = lane < kdim
    lane16 = lax.broadcasted_iota(jnp.int32, (16, 2 * kdim), 1)
    group = (lane16 // rank) % rep

    p_copies, e_copies = [], []

    def project(s):
        rows = pl.ds(s * LEN, LEN)
        hid_loads[s].wait()
        if s == 0:
            for c in w_loads[:1 + rep]:
                c.wait()
        from_in = lax.dot_general(hid_v[rows, :], left_v[...], CONTRACT_LAST, preferred_element_type=f32)
        grad_loads[s].wait()
        if s == 0:
            for c in w_loads[1 + rep:]:
                c.wait()
        from_gr = lax.dot_general(grad_v[rows, :], right_v[...], CONTRACT_LAST, preferred_element_type=f32)
        a = jnp.where(low, from_in, from_gr)
        b = jnp.where(low, from_gr, from_in)
        own_a[s] = a
        for j in range(nt):
            at = j * block
            packed = jnp.zeros((16, 2 * kdim), f32)
            for i in range(pack):
                packed = jnp.where(group == i, b[at + 16 * i:at + 16 * i + 16], packed)
            own_b[s, j] = packed
            send_p[s, j, pl.ds(0, block), :] = a[at:at + block].astype(WIRE)
            packed_hi = packed.astype(WIRE)
            send_p[s, j, pl.ds(block, 16), :] = packed_hi
            send_p[s, j, pl.ds(block + 16, 16), :] = (packed - packed_hi.astype(f32)).astype(WIRE)
        if s == 0:
            pl.semaphore_wait(barrier, nd * nt - 1)
        copies = []
        for k in range(1, nt):
            to = lax.rem(t + k, nt)
            c = pltpu.make_async_remote_copy(
                src_ref=send_p.at[s, to], dst_ref=recv_p.at[s, k - 1],
                send_sem=p_send.at[s, k - 1], recv_sem=p_recv.at[s, k - 1],
                device_id=(part, d, to), device_id_type=MESH,
            )
            c.start()
            copies.append(c)
        p_copies.append(copies)

    def bilinear(s):
        for c in p_copies[s]:
            c.wait_recv()
        a = own_a[s, pl.ds(pl.multiple_of(t * block, block), block), :]
        b = own_b[s, t]
        for k in range(nt - 1):
            a = a + recv_p[s, k, pl.ds(0, block), :].astype(f32)
            b = b + recv_p[s, k, pl.ds(block, 16), :].astype(f32)
            b = b + recv_p[s, k, pl.ds(block + 16, 16), :].astype(f32)
        b = jnp.concatenate([jnp.where(group == i, b, 0.0) for i in range(pack)], 0)
        a_hi, b_hi = a.astype(bf16), b.astype(bf16)
        a_lo = (a - a_hi.astype(f32)).astype(bf16)
        b_lo = (b - b_hi.astype(f32)).astype(bf16)
        z = lax.dot_general(
            jnp.concatenate([b_hi, b_lo, b_hi], 0), jnp.concatenate([a_hi, a_hi, a_lo], 0),
            CONTRACT_FIRST, preferred_element_type=f32,
        )
        va, ub = z[0:rank], z[kdim:kdim + rank]
        for i in range(1, pack):
            va = va + z[rank * i:rank * i + rank]
            ub = ub + z[kdim + rank * i:kdim + rank * i + rank]
        own_e[s] = jnp.where(lane16 < kdim, va, ub)
        copies = []
        for k in range(1, nt):
            to = lax.rem(t + k, nt)
            c = pltpu.make_async_remote_copy(
                src_ref=own_e.at[s], dst_ref=recv_e.at[k - 1, s],
                send_sem=e_send.at[s, k - 1], recv_sem=e_recv.at[s, k - 1],
                device_id=(part, d, to), device_id_type=MESH,
            )
            c.start()
            copies.append(c)
        e_copies.append(copies)

    for s in range(seqs):
        project(s)
        if s >= 2:
            bilinear(s - 2)
    for s in range(max(seqs - 2, 0), seqs):
        bilinear(s)

    half = rank * kdim
    rows_e = 2 * seqs * rank
    col = lax.broadcasted_iota(jnp.int32, (2 * kdim, width), 1) + t * width
    lane_of = jnp.where(col < half, kdim + col // rank, (col - half) % kdim)
    pick = (lax.broadcasted_iota(jnp.int32, (2 * kdim, width), 0) == lane_of).astype(bf16)
    colr = lax.broadcasted_iota(jnp.int32, (rows_e, width), 1) + t * width
    row_of = jnp.where(colr < half, colr % rank, (colr - half) // kdim)
    keep = (lax.broadcasted_iota(jnp.int32, (rows_e, width), 0) % rank) == row_of
    fold = (
        (lax.broadcasted_iota(jnp.int32, (8, rows_e), 1) // rank) % seqs
        == lax.broadcasted_iota(jnp.int32, (8, rows_e), 0)
    ).astype(bf16)

    for copies in e_copies:
        for c in copies:
            c.wait_recv()
    e = own_e[...]
    for k in range(nt - 1):
        e = e + recv_e[k]
    e = split(e.reshape(seqs * rank, 2 * kdim))
    spread = jnp.dot(e, pick, preferred_element_type=f32)
    spread = jnp.where(keep, spread, 0.0).astype(bf16)
    example = jnp.dot(fold, spread, preferred_element_type=f32)
    own_s[...] = example
    s_copies = []
    for k in range(1, nd):
        c = pltpu.make_async_remote_copy(
            src_ref=own_s, dst_ref=all_s.at[k - 1],
            send_sem=s_send.at[k - 1], recv_sem=s_recv.at[k - 1],
            device_id=(part, lax.rem(d + k, nd), t), device_id_type=MESH,
        )
        c.start()
        s_copies.append(c)
    t_load.wait()

    for c in s_copies:
        c.wait_recv()
    stacked = split(jnp.concatenate([example] + [all_s[k] for k in range(nd - 1)], 0))
    scores = lax.dot_general(stacked, tests_v[...], CONTRACT_LAST, preferred_element_type=f32)
    scores = scores[:8 * nd] + scores[8 * nd:]
    per = nd // nt
    home = d // per
    slot = lax.rem(d, per)
    part_s[...] = scores.reshape(part_s.shape)

    def send_scores(k):
        to = lax.rem(d + nd - k, nd)
        return pltpu.make_async_remote_copy(
            src_ref=part_s.at[k], dst_ref=recv_s.at[slot, t],
            send_sem=o_send.at[k], recv_sem=o_recv.at[slot, t],
            device_id=(part, to, home), device_id_type=MESH,
        )

    for k in range(nd):
        if k == 0:
            @pl.when(home != t)
            def _():
                send_scores(0).start()

            @pl.when(home == t)
            def _():
                recv_s[slot, t] = part_s[0]
        else:
            send_scores(k).start()

    for j in range(per):
        total = None
        for i in range(nt):
            local = jnp.logical_and(t * per + j == d, i == t)

            @pl.when(jnp.logical_not(local))
            def _():
                pltpu.make_async_remote_copy(
                    src_ref=part_s.at[0], dst_ref=recv_s.at[j, i],
                    send_sem=o_send.at[0], recv_sem=o_recv.at[j, i],
                    device_id=(part, d, t), device_id_type=MESH,
                ).wait_recv()
            total = recv_s[j, i] if total is None else total + recv_s[j, i]
        tests_here = tests.shape[0]
        out[:, j * tests_here:(j + 1) * tests_here] = total[:seqs]

    for copies in p_copies + e_copies + [s_copies]:
        for c in copies:
            c.wait_send()
    for k in range(nd):
        if k == 0:
            @pl.when(home != t)
            def _():
                send_scores(0).wait_send()
        else:
            send_scores(k).wait_send()


def solution(mesh):
    nd, nt = mesh.shape["dp"], mesh.shape["tensor"]

    def body(hidden, outgrad, down, inproj, up, outproj, tests):
        rows, hid = hidden.shape
        feat = outgrad.shape[1]
        rank, kdim = down.shape[0], inproj.shape[0]
        seqs = rows // LEN
        block = LEN // nt
        tests_here, width = tests.shape
        per = nd // nt
        f32, bf16 = jnp.float32, jnp.bfloat16
        lanes = 2 * kdim
        rep = kdim // rank
        dma = pltpu.SemaphoreType.DMA
        return pl.pallas_call(
            functools.partial(kernel, (nd, nt)),
            out_shape=jax.ShapeDtypeStruct((seqs, tests_here * per), f32),
            in_specs=[pl.BlockSpec(memory_space=pl.ANY)] * 7,
            out_specs=pl.BlockSpec(memory_space=pltpu.VMEM),
            scratch_shapes=[
                pltpu.VMEM((rows, hid), bf16),
                pltpu.VMEM((rows, feat), bf16),
                pltpu.VMEM((lanes, hid), bf16),
                pltpu.VMEM((lanes, feat), bf16),
                pltpu.VMEM((tests_here, width), bf16),
                pltpu.VMEM((seqs, LEN, lanes), f32),
                pltpu.VMEM((seqs, nt, 16, lanes), f32),
                pltpu.VMEM((seqs, nt, block + 32, lanes), WIRE),
                pltpu.VMEM((seqs, nt - 1, block + 32, lanes), WIRE),
                pltpu.VMEM((seqs, rank, lanes), f32),
                pltpu.VMEM((nt - 1, seqs, rank, lanes), f32),
                pltpu.VMEM((8, width), f32),
                pltpu.VMEM((nd - 1, 8, width), f32),
                pltpu.VMEM((nd, 8, tests_here), f32),
                pltpu.VMEM((per, nt, 8, tests_here), f32),
                dma((seqs,)), dma((seqs,)), dma((2 + 2 * rep,)), dma,
                dma((seqs, nt - 1)), dma((seqs, nt - 1)),
                dma((seqs, nt - 1)), dma((seqs, nt - 1)),
                dma((nd - 1,)), dma((nd - 1,)),
                dma((nd,)), dma((per, nt)),
            ],
            compiler_params=pltpu.CompilerParams(
                collective_id=0, has_side_effects=True, vmem_limit_bytes=56 * 1024 * 1024,
            ),
            cost_estimate=pl.CostEstimate(
                flops=2 * rows * (hid + feat) * lanes,
                bytes_accessed=2 * rows * (hid + feat), transcendentals=0,
            ),
        )(hidden, outgrad, down, inproj, up.T, outproj, tests)

    return jax.shard_map(
        body,
        mesh=mesh,
        in_specs=(
            P(("parts", "dp"), "tensor"),
            P(("parts", "dp"), "tensor"),
            P(None, "tensor"),
            P(None, "tensor"),
            P("tensor", None),
            P(None, "tensor"),
            P("dp", "tensor"),
        ),
        out_specs=P(("parts", "dp"), "tensor"),
        check_vma=False,
    )
```

time: 109 us -> 46 us (0.42)
  the two profiles are of different devices: /device:TPU:0 before, /device:TPU:1 now
where the time goes in v1:
time: 46 us; the launch traced here: 45.8 us
  Pallas kernels  44.4 us (97%)
  local copies, waits for them, and re-layouts  1.38 us (3%)
    pallas_call x1, Pallas kernels, body(): pl.pallas_call(functools.partial(kernel, (nd, nt)), out_shape=jax.ShapeDt...  44.4 us
    unnamed x1, local copies, waits for them, and re-layouts  1.38 us

profile of v1, /device:TPU:1, one launch (start us, length us, event | category | flops | bytes accessed | tf_op | source)
XLA Modules:
  0.0 45.8 jit_solution(3292263789299426151)
XLA Ops:
  0.0 44.4 %shard_map.73 = f32[5,1024]{1,0:T(8,128)} custom-call(bf16[1280,7168]{1,0:T(8,128)(2,1)} %hidden.1, bf16[1280,2048]{1,0:T(8,128)(2,1)} %outgrad.1, bf16[16,7168]{1,0:T(8,128)(2,1)} %down.1, bf16[64,7168]{1,0:T(8,128)(2,1)} %inproj.1, bf16[16,2048]{1,0:T(8,128)(2,1)} %bitcast.1, bf16[64,2048]{1,0:T(8,128)(2,1)} %outproj.1, bf16[1024,512]{1,0:T(8,128)(2,1)} %tests.1), custom_call_target="tpu_custom_call" | custom-call | flops 3019898880 | bytes 23592960 | tf_op jit(solution)/shard_map/pallas_call | solution.py:270
  44.4 1.4 %copy.9 = f32[5,1024]{1,0:T(8,128)} copy(f32[5,1024]{1,0:T(8,128)} %shard_map.73) | data formatting | bytes 40960

commit v2 on v1

--- a/solution.py
+++ b/solution.py
@@ -8,6 +8,8 @@
 from jax.sharding import PartitionSpec as P
 
 LEN = 256
+PIECES = 3
+AHEAD = 3
 MESH = pl.DeviceIdType.MESH
 WIRE = jnp.bfloat16
 CONTRACT_LAST = (((1,), (1,)), ((), ()))
@@ -48,19 +50,35 @@
         copy.start()
         return copy
 
-    w_loads = [load(inproj, left_v.at[pl.ds(0, kdim)], w_sem.at[0])]
-    for i in range(rep):
-        w_loads.append(load(down, left_v.at[pl.ds(kdim + rank * i, rank)], w_sem.at[1 + i]))
-    hid_loads, grad_loads = [], []
+    w_loads = [
+        load(inproj, left_v.at[pl.ds(0, kdim)], w_sem.at[0]),
+        load(down, left_v.at[pl.ds(kdim, rank)], w_sem.at[1]),
+    ]
+    hid = hidden.shape[1]
+    cut = hid // (PIECES - 1)
+    pieces = []
     for s in range(seqs):
         rows = pl.ds(s * LEN, LEN)
-        hid_loads.append(load(hidden.at[rows], hid_v.at[rows], hid_sem.at[s]))
-        if s == 0:
-            for i in range(rep):
-                w_loads.append(load(up_t, right_v.at[pl.ds(rank * i, rank)], w_sem.at[1 + rep + i]))
-            w_loads.append(load(outproj, right_v.at[pl.ds(kdim, kdim)], w_sem.at[1 + 2 * rep]))
-        grad_loads.append(load(outgrad.at[rows], grad_v.at[rows], grad_sem.at[s]))
-    t_load = load(tests, tests_v, t_sem)
+        for i in range(PIECES - 1):
+            cols = pl.ds(i * cut, cut)
+            pieces.append((hidden.at[rows, cols], hid_v.at[rows, cols], hid_sem.at[s, i]))
+        pieces.append((outgrad.at[rows], grad_v.at[rows], grad_sem.at[s]))
+    pieces.append((tests, tests_v, t_sem))
+    reads = []
+
+    def read_next():
+        if len(reads) < len(pieces):
+            reads.append(load(*pieces[len(reads)]))
+
+    def arrive(n):
+        reads[n].wait()
+        read_next()
+
+    for i in range(AHEAD):
+        read_next()
+        if i == 0:
+            w_loads.append(load(up_t, right_v.at[pl.ds(0, rank)], w_sem.at[2]))
+            w_loads.append(load(outproj, right_v.at[pl.ds(kdim, kdim)], w_sem.at[3]))
 
     barrier = pltpu.get_barrier_semaphore()
     for kd in range(nd):
@@ -81,15 +99,23 @@
 
     def project(s):
         rows = pl.ds(s * LEN, LEN)
-        hid_loads[s].wait()
         if s == 0:
-            for c in w_loads[:1 + rep]:
+            for c in w_loads[:2]:
                 c.wait()
-        from_in = lax.dot_general(hid_v[rows, :], left_v[...], CONTRACT_LAST, preferred_element_type=f32)
-        grad_loads[s].wait()
+            for i in range(1, rep):
+                left_v[pl.ds(kdim + rank * i, rank), :] = left_v[pl.ds(kdim, rank), :]
+        from_in = None
+        for i in range(PIECES - 1):
+            cols = pl.ds(i * cut, cut)
+            arrive(s * PIECES + i)
+            term = lax.dot_general(hid_v[rows, cols], left_v[:, cols], CONTRACT_LAST, preferred_element_type=f32)
+            from_in = term if from_in is None else from_in + term
+        arrive(s * PIECES + PIECES - 1)
         if s == 0:
-            for c in w_loads[1 + rep:]:
+            for c in w_loads[2:]:
                 c.wait()
+            for i in range(1, rep):
+                right_v[pl.ds(rank * i, rank), :] = right_v[pl.ds(0, rank), :]
         from_gr = lax.dot_general(grad_v[rows, :], right_v[...], CONTRACT_LAST, preferred_element_type=f32)
         a = jnp.where(low, from_in, from_gr)
         b = jnp.where(low, from_gr, from_in)
@@ -192,7 +218,7 @@
         )
         c.start()
         s_copies.append(c)
-    t_load.wait()
+    reads[-1].wait()
 
     for c in s_copies:
         c.wait_recv()
@@ -207,7 +233,7 @@
     def send_scores(k):
         to = lax.rem(d + nd - k, nd)
         return pltpu.make_async_remote_copy(
-            src_ref=part_s.at[k], dst_ref=recv_s.at[slot, t],
+            src_ref=part_s.at[k, pl.ds(0, seqs)], dst_ref=recv_s.at[slot, t, pl.ds(0, seqs)],
             send_sem=o_send.at[k], recv_sem=o_recv.at[slot, t],
             device_id=(part, to, home), device_id_type=MESH,
         )
@@ -220,7 +246,7 @@
 
             @pl.when(home == t)
             def _():
-                recv_s[slot, t] = part_s[0]
+                recv_s[slot, t, pl.ds(0, seqs), :] = part_s[0, pl.ds(0, seqs), :]
         else:
             send_scores(k).start()
 
@@ -232,13 +258,14 @@
             @pl.when(jnp.logical_not(local))
             def _():
                 pltpu.make_async_remote_copy(
-                    src_ref=part_s.at[0], dst_ref=recv_s.at[j, i],
+                    src_ref=part_s.at[0, pl.ds(0, seqs)], dst_ref=recv_s.at[j, i, pl.ds(0, seqs)],
                     send_sem=o_send.at[0], recv_sem=o_recv.at[j, i],
                     device_id=(part, d, t), device_id_type=MESH,
                 ).wait_recv()
-            total = recv_s[j, i] if total is None else total + recv_s[j, i]
+            here = recv_s[j, i, pl.ds(0, seqs), :]
+            total = here if total is None else total + here
         tests_here = tests.shape[0]
-        out[:, j * tests_here:(j + 1) * tests_here] = total[:seqs]
+        out[:, j * tests_here:(j + 1) * tests_here] = total
 
     for copies in p_copies + e_copies + [s_copies]:
         for c in copies:
@@ -288,7 +315,7 @@
                 pltpu.VMEM((nd - 1, 8, width), f32),
                 pltpu.VMEM((nd, 8, tests_here), f32),
                 pltpu.VMEM((per, nt, 8, tests_here), f32),
-                dma((seqs,)), dma((seqs,)), dma((2 + 2 * rep,)), dma,
+                dma((seqs, PIECES - 1)), dma((seqs,)), dma((4,)), dma,
                 dma((seqs, nt - 1)), dma((seqs, nt - 1)),
                 dma((seqs, nt - 1)), dma((seqs, nt - 1)),
                 dma((nd - 1,)), dma((nd - 1,)),

time: 46 us -> 40.2 us (0.87)
  Pallas kernels: 44.4 us -> 38.7 us
    pallas_call x1, Pallas kernels: 44.4 us -> 38.7 us  [body(): pl.pallas_call(functools.partial(kernel, (nd, nt)), out_shape=jax.ShapeDt...]
where the time goes in v2:
time: 40.2 us; the launch traced here: 40 us
  Pallas kernels  38.7 us (96%)
  local copies, waits for them, and re-layouts  1.38 us (3%)
    pallas_call x1, Pallas kernels, body(): pl.pallas_call(functools.partial(kernel, (nd, nt)), out_shape=jax.ShapeDt...  38.7 us
    unnamed x1, local copies, waits for them, and re-layouts  1.38 us

profile of v2, /device:TPU:1, one launch (start us, length us, event | category | flops | bytes accessed | tf_op | source)
XLA Modules:
  0.0 40.0 jit_solution(4003671862330857240)
XLA Ops:
  0.0 38.7 %shard_map.73 = f32[5,1024]{1,0:T(8,128)} custom-call(bf16[1280,7168]{1,0:T(8,128)(2,1)} %hidden.1, bf16[1280,2048]{1,0:T(8,128)(2,1)} %outgrad.1, bf16[16,7168]{1,0:T(8,128)(2,1)} %down.1, bf16[64,7168]{1,0:T(8,128)(2,1)} %inproj.1, bf16[16,2048]{1,0:T(8,128)(2,1)} %bitcast.1, bf16[64,2048]{1,0:T(8,128)(2,1)} %outproj.1, bf16[1024,512]{1,0:T(8,128)(2,1)} %tests.1), custom_call_target="tpu_custom_call" | custom-call | flops 3019898880 | bytes 23592960 | tf_op jit(solution)/shard_map/pallas_call | solution.py:297
  38.7 1.4 %copy.9 = f32[5,1024]{1,0:T(8,128)} copy(f32[5,1024]{1,0:T(8,128)} %shard_map.73) | data formatting | bytes 40960

commit v3 on v2

--- a/solution.py
+++ b/solution.py
@@ -8,8 +8,8 @@
 from jax.sharding import PartitionSpec as P
 
 LEN = 256
-PIECES = 3
-AHEAD = 3
+PIECES = 2
+AHEAD = 4
 MESH = pl.DeviceIdType.MESH
 WIRE = jnp.bfloat16
 CONTRACT_LAST = (((1,), (1,)), ((), ()))
@@ -180,9 +180,9 @@
 
     for s in range(seqs):
         project(s)
-        if s >= 2:
-            bilinear(s - 2)
-    for s in range(max(seqs - 2, 0), seqs):
+        if s >= 3:
+            bilinear(s - 3)
+    for s in range(max(seqs - 3, 0), seqs):
         bilinear(s)
 
     half = rank * kdim

time: 40.2 us -> 39.2 us (0.975)
  Pallas kernels: 38.7 us -> 37.7 us
    pallas_call x1, Pallas kernels: 38.7 us -> 37.7 us  [body(): pl.pallas_call(functools.partial(kernel, (nd, nt)), out_shape=jax.ShapeDt...]
where the time goes in v3:
time: 39.2 us; the launch traced here: 39 us
  Pallas kernels  37.7 us (96%)
  local copies, waits for them, and re-layouts  1.38 us (4%)
    pallas_call x1, Pallas kernels, body(): pl.pallas_call(functools.partial(kernel, (nd, nt)), out_shape=jax.ShapeDt...  37.7 us
    unnamed x1, local copies, waits for them, and re-layouts  1.38 us

profile of v3, /device:TPU:1, one launch (start us, length us, event | category | flops | bytes accessed | tf_op | source)
XLA Modules:
  0.0 39.0 jit_solution(14723543928233204156)
XLA Ops:
  0.0 37.7 %shard_map.73 = f32[5,1024]{1,0:T(8,128)} custom-call(bf16[1280,7168]{1,0:T(8,128)(2,1)} %hidden.1, bf16[1280,2048]{1,0:T(8,128)(2,1)} %outgrad.1, bf16[16,7168]{1,0:T(8,128)(2,1)} %down.1, bf16[64,7168]{1,0:T(8,128)(2,1)} %inproj.1, bf16[16,2048]{1,0:T(8,128)(2,1)} %bitcast.1, bf16[64,2048]{1,0:T(8,128)(2,1)} %outproj.1, bf16[1024,512]{1,0:T(8,128)(2,1)} %tests.1), custom_call_target="tpu_custom_call" | custom-call | flops 3019898880 | bytes 23592960 | tf_op jit(solution)/shard_map/pallas_call | solution.py:297
  37.7 1.4 %copy.9 = f32[5,1024]{1,0:T(8,128)} copy(f32[5,1024]{1,0:T(8,128)} %shard_map.73) | data formatting | bytes 40960
